TPU v7x, 32 devices: a whole 2x2x4 slice. The times are simulated.
32 devices in a mesh: groups: 2 (over y), gx: 16 (over z, x, core).
Axes of the slice: x: 2, y: 2, z: 4, core: 2. Of those that a mesh axis runs over, the one named last changes fastest.
Arguments:
- tokens: bfloat16 [640, 8192], P('groups', 'gx'), parts along dimension 0, may hold values from -180 to 180, as said below
- norm_gain: bfloat16 [8192], P('gx'), may hold values from 0.25 to 1.75
- gate_weight: bfloat16 [16, 2048, 7168], P('gx'), may hold values from -0.0625 to 0.0625
- up_weight: bfloat16 [16, 2048, 7168], P('gx'), may hold values from -0.0625 to 0.0625
- down_weight: bfloat16 [16, 7168, 2048], P('gx'), may hold values from -0.03125 to 0.03125
Outputs:
- mixed: bfloat16 [640, 8192], P('groups', 'gx'), parts along dimension 0
There are 2 independent parts, one for each index of `groups`. A program takes and returns all parts, laid end to end along the dimension named above; an argument that names none is the same for every part. Nothing has to cross between parts.
Inputs may be any that keep to these rules, and one draw needn't show every extreme that they name: `tokens`: hidden states with scales that differ between rows and between features.
All inputs are finite; a program needn't handle non-finite values.
Results may differ from a plain program's by a relative error of at most 0.0065.
Values may be sent and summed in bfloat16 or wider, within the bound.
A program may use at most 320 MiB of HBM per device.

v0:
```python
import jax
import jax.numpy as jnp
from jax import lax
from jax.sharding import PartitionSpec as P

D = 8192


epsilon = 1e-05


def partner(block, axis, distance):
    count = lax.axis_size(axis)
    route = []
    for low in range(count):
        high = low | 1 << distance
        if high != low and high < count:
            route += [(low, high), (high, low)]
    return lax.ppermute(block, axis, route)


def per_device(tokens, norm_gain, gate_weight, up_weight, down_weight):
    total_bits = lax.axis_size("gx").bit_length() - 1
    low_bits = (total_bits + 1) // 2
    position = lax.axis_index("gx")
    gate_tile = gate_weight[0]
    up_tile = up_weight[0]
    down_tile = down_weight[0]
    narrowed = tokens.astype(jnp.float32)
    totals = lax.psum(jnp.sum(narrowed * narrowed, axis=1), "gx")
    scaling = lax.rsqrt(totals / D + epsilon)[:, None]
    normed = (narrowed * scaling * norm_gain.astype(jnp.float32)).astype(jnp.bfloat16)
    block = normed
    for bit in range(low_bits):
        other = partner(block, "gx", bit)
        upper = position >> bit & 1 == 1
        block = jnp.where(
            upper, jnp.concatenate([other, block], 1), jnp.concatenate([block, other], 1)
        )
    gate_part = jnp.dot(block, gate_tile, preferred_element_type=jnp.float32)
    up_part = jnp.dot(block, up_tile, preferred_element_type=jnp.float32)
    stacked = jnp.stack([gate_part, up_part])
    for bit in reversed(range(low_bits, total_bits)):
        half = stacked.shape[2] // 2
        lower_half = stacked[:, :, :half]
        upper_half = stacked[:, :, half:]
        upper = position >> bit & 1 == 1
        keeping = jnp.where(upper, upper_half, lower_half)
        sending = jnp.where(upper, lower_half, upper_half)
        stacked = keeping + partner(sending, "gx", bit)
    hidden = (jax.nn.silu(stacked[0]) * stacked[1]).astype(jnp.bfloat16)
    for bit in range(low_bits, total_bits):
        other = partner(hidden, "gx", bit)
        upper = position >> bit & 1 == 1
        hidden = jnp.where(
            upper, jnp.concatenate([other, hidden], 1), jnp.concatenate([hidden, other], 1)
        )
    partial_value = jnp.dot(hidden, down_tile, preferred_element_type=jnp.float32)
    for bit in reversed(range(low_bits)):
        half = partial_value.shape[1] // 2
        lower_half = partial_value[:, :half]
        upper_half = partial_value[:, half:]
        upper = position >> bit & 1 == 1
        keeping = jnp.where(upper, upper_half, lower_half)
        sending = jnp.where(upper, lower_half, upper_half)
        partial_value = keeping + partner(sending, "gx", bit)
    return partial_value.astype(jnp.bfloat16)


def solution(mesh):
    placed = (
        P("groups", "gx"),
        P("gx"),
        P("gx", None, None),
        P("gx", None, None),
        P("gx", None, None),
    )
    return jax.shard_map(
        per_device, mesh=mesh, in_specs=placed, out_specs=P("groups", "gx"), check_vma=False
    )
```

profile of v0, /device:TPU:0, one launch (start us, length us, event | category | flops | bytes accessed | tf_op | source)
XLA Modules:
  0.0 792.3 jit_solution(7075681567931805706)
XLA Ops:
  0.0 0.7 convert_element_type.16
  0.7 1.1 fusion.21
  1.8 34.9 %psum.7 = f32[320]{0:T(512)S(1)} all-reduce(f32[320]{0:T(512)S(1)} %fusion.21), channel_id=1, replica_groups=mesh['groups'=2,'gx'=16] {'gx'}, use_global_device_ids=true, to_apply=%region_1.0 | all-reduce | flops 320 | bytes 2560 | tf_op jit(solution)/shard_map/psum | solution.py:30
  36.7 1.1 fusion.23
  37.8 0.1 collective-permute-start
  37.9 1.6 collective-permute-done
  39.5 0.2 maximum_select_fusion.4
  39.7 0.1 collective-permute-start.1
  39.8 16.9 %collective-permute-done.1 = bf16[320,1024]{1,0:T(8,128)(2,1)} collective-permute-done((bf16[320,1024]{1,0:T(8,128)(2,1)S(1)}, bf16[320,1024]{1,0:T(8,128)(2,1)}, u32[]{:S(2)}, u32[]{:S(2)}) %collective-permute-start.1) | collective-permute-done | bytes 655392 | tf_op jit(solution)/shard_map/ppermute | solution.py:19
  56.7 18.1 %fusion.9 = f32[1,320,7168]{2,1,0:T(8,128)S(1)} fusion(bf16[1,2048,7168]{2,1,0:T(8,128)(2,1)} %param.8, bf16[320,1024]{1,0:T(8,128)(2,1)S(1)} %maximum_select_fusion.4, bf16[320,1024]{1,0:T(8,128)(2,1)} %collective-permute-done.1, pred[]{:T(512)S(6)} %eq.17), kind=kOutput, calls=%fused_computation.9 | convolution fusion | flops 9401139200 | bytes 39845888 | tf_op jit(solution)/shard_map/dot_general | solution.py:41
  74.7 0.0 copy-start
  74.7 21.7 %fusion.6 = f32[1,320,7168]{2,1,0:T(8,128)} fusion(bf16[1,2048,7168]{2,1,0:T(8,128)(2,1)} %param.7, bf16[320,1024]{1,0:T(8,128)(2,1)S(1)} %maximum_select_fusion.4, bf16[320,1024]{1,0:T(8,128)(2,1)} %collective-permute-done.1, pred[]{:T(512)S(6)} %eq.17), kind=kOutput, calls=%fused_computation.8 | convolution fusion | flops 9401139200 | bytes 39845888 | tf_op jit(solution)/shard_map/dot_general | solution.py:40
  96.4 0.0 copy-done
  96.4 6.7 broadcast_select_fusion
  103.1 0.0 collective-permute-start.2
  103.1 392.8 %collective-permute-done.2 = f32[2,320,3584]{2,1,0:T(8,128)} collective-permute-done((f32[2,320,3584]{2,1,0:T(8,128)}, f32[2,320,3584]{2,1,0:T(8,128)}, u32[]{:S(2)}, u32[]{:S(2)}) %collective-permute-start.2) | collective-permute-done | bytes 9175072 | tf_op jit(solution)/shard_map/ppermute | solution.py:19
  495.9 10.2 %select_add_fusion = f32[2,320,3584]{2,1,0:T(8,128)S(1)} fusion(f32[2,320,3584]{2,1,0:T(8,128)} %collective-permute-done.2, pred[]{:T(512)S(6)} %eq.18, f32[1,320,7168]{2,1,0:T(8,128)} %copy-done, f32[1,320,7168]{2,1,0:T(8,128)} %fusion.6), kind=kLoop, calls=%fused_computation.12 | loop fusion | flops 9175040 | bytes 36700160 | tf_op jit(solution)/shard_map/add | solution.py:50
  506.1 0.5 slice_select_fusion
  506.7 0.1 collective-permute-start.3
  506.7 100.9 %collective-permute-done.3 = f32[2,320,1792]{2,1,0:T(8,128)S(1)} collective-permute-done((f32[2,320,1792]{2,1,0:T(8,128)S(1)}, f32[2,320,1792]{2,1,0:T(8,128)S(1)}, u32[]{:S(2)}, u32[]{:S(2)}) %collective-permute-start.3) | collective-permute-done | bytes 4587552 | tf_op jit(solution)/shard_map/ppermute | solution.py:19
  607.7 0.8 select_add_fusion.1
  608.5 0.7 fusion.20
  609.2 0.4 collective-permute-start.4
  609.5 26.1 %collective-permute-done.4 = bf16[320,1792]{1,0:T(8,128)(2,1)S(1)} collective-permute-done((bf16[320,1792]{1,0:T(8,128)(2,1)S(1)}, bf16[320,1792]{1,0:T(8,128)(2,1)S(1)}, u32[]{:S(2)}, u32[]{:S(2)}) %collective-permute-start.4) | collective-permute-done | bytes 1146912 | tf_op jit(solution)/shard_map/ppermute | solution.py:19
  635.6 0.5 maximum_select_fusion.2
  636.1 0.0 copy-start.1
  636.1 0.1 collective-permute-start.5
  636.2 1.3 copy-done.1
  637.5 98.8 %collective-permute-done.5 = bf16[320,3584]{1,0:T(8,128)(2,1)} collective-permute-done((bf16[320,3584]{1,0:T(8,128)(2,1)S(1)}, bf16[320,3584]{1,0:T(8,128)(2,1)}, u32[]{:S(2)}, u32[]{:S(2)}) %collective-permute-start.5) | collective-permute-done | bytes 2293792 | tf_op jit(solution)/shard_map/ppermute | solution.py:19
  736.4 21.8 %fusion = f32[320,2048]{1,0:T(8,128)S(1)} fusion(bf16[1,7168,2048]{2,1,0:T(8,128)(2,1)} %param.9, bf16[320,3584]{1,0:T(8,128)(2,1)} %copy-done.1, bf16[320,3584]{1,0:T(8,128)(2,1)} %collective-permute-done.5, pred[]{:T(512)S(6)} %eq.18), kind=kOutput, calls=%fused_computation | convolution fusion | flops 9415884800 | bytes 36569088 | tf_op jit(solution)/shard_map/dot_general | solution.py:58
  758.2 0.2 slice_select_fusion.1
  758.4 1.6 collective-permute-start.6
  760.0 28.8 %collective-permute-done.6 = f32[320,1024]{1,0:T(8,128)S(1)} collective-permute-done((f32[320,1024]{1,0:T(8,128)S(1)}, f32[320,1024]{1,0:T(8,128)S(1)}, u32[]{:S(2)}, u32[]{:S(2)}) %collective-permute-start.6) | collective-permute-done | bytes 1310752 | tf_op jit(solution)/shard_map/ppermute | solution.py:19
  788.7 0.4 select_add_fusion.2
  789.1 0.1 slice_select_fusion.2
  789.2 0.1 collective-permute-start.7
  789.3 2.1 collective-permute-done.7
  791.4 0.9 add_convert_fusion
  (1 shorter events, 0.0 us)
Async XLA Ops:
  37.8 1.7 collective-permute-start
  39.7 16.9 %collective-permute-start.1 = (bf16[320,1024]{1,0:T(8,128)(2,1)S(1)}, bf16[320,1024]{1,0:T(8,128)(2,1)}, u32[]{:S(2)}, u32[]{:S(2)}) collective-permute-start(bf16[320,1024]{1,0:T(8,128)(2,1)S(1)} %maximum_select_fusion.4), channel_id=1, source_target_pairs={{0,2},{2,0},{1,3},{3,1},{4,6},{6,4},{5,7},{7,5},{8,10},{10,8},{9,1... | collective-permute-start | bytes 1966088 | tf_op jit(solution)/shard_map/ppermute | solution.py:19
  74.7 21.7 %copy-start = (f32[1,320,7168]{2,1,0:T(8,128)}, f32[1,320,7168]{2,1,0:T(8,128)S(1)}, u32[]{:S(2)}) copy-start(f32[1,320,7168]{2,1,0:T(8,128)S(1)} %fusion.9) | copy-start | bytes 27525124
  103.1 392.8 %collective-permute-start.2 = (f32[2,320,3584]{2,1,0:T(8,128)}, f32[2,320,3584]{2,1,0:T(8,128)}, u32[]{:S(2)}, u32[]{:S(2)}) collective-permute-start(f32[2,320,3584]{2,1,0:T(8,128)} %broadcast_select_fusion), channel_id=1, source_target_pairs={{0,8},{8,0},{1,9},{9,1},{2,10},{10,2},{3,11},{11,3},{4,12},{12,4},... | collective-permute-start | bytes 27525128 | tf_op jit(solution)/shard_map/ppermute | solution.py:19
  506.7 101.0 %collective-permute-start.3 = (f32[2,320,1792]{2,1,0:T(8,128)S(1)}, f32[2,320,1792]{2,1,0:T(8,128)S(1)}, u32[]{:S(2)}, u32[]{:S(2)}) collective-permute-start(f32[2,320,1792]{2,1,0:T(8,128)S(1)} %slice_select_fusion), channel_id=1, source_target_pairs={{0,4},{4,0},{1,5},{5,1},{2,6},{6,2},{3,7},{7,3},{8,12},{12,8},{9,1... | collective-permute-start | bytes 13762568 | tf_op jit(solution)/shard_map/ppermute | solution.py:19
  609.2 26.4 %collective-permute-start.4 = (bf16[320,1792]{1,0:T(8,128)(2,1)S(1)}, bf16[320,1792]{1,0:T(8,128)(2,1)S(1)}, u32[]{:S(2)}, u32[]{:S(2)}) collective-permute-start(bf16[320,1792]{1,0:T(8,128)(2,1)S(1)} %fusion.20), channel_id=1, source_target_pairs={{0,4},{4,0},{1,5},{5,1},{2,6},{6,2},{3,7},{7,3},{8,12},{12,8},{9,1... | collective-permute-start | bytes 3440648 | tf_op jit(solution)/shard_map/ppermute | solution.py:19
  636.1 1.4 copy-start.1
  636.1 100.2 %collective-permute-start.5 = (bf16[320,3584]{1,0:T(8,128)(2,1)S(1)}, bf16[320,3584]{1,0:T(8,128)(2,1)}, u32[]{:S(2)}, u32[]{:S(2)}) collective-permute-start(bf16[320,3584]{1,0:T(8,128)(2,1)S(1)} %maximum_select_fusion.2), channel_id=1, source_target_pairs={{0,8},{8,0},{1,9},{9,1},{2,10},{10,2},{3,11},{11,3},{4,12},{12,4},... | collective-permute-start | bytes 6881288 | tf_op jit(solution)/shard_map/ppermute | solution.py:19
  758.4 30.3 %collective-permute-start.6 = (f32[320,1024]{1,0:T(8,128)S(1)}, f32[320,1024]{1,0:T(8,128)S(1)}, u32[]{:S(2)}, u32[]{:S(2)}) collective-permute-start(f32[320,1024]{1,0:T(8,128)S(1)} %slice_select_fusion.1), channel_id=1, source_target_pairs={{0,2},{2,0},{1,3},{3,1},{4,6},{6,4},{5,7},{7,5},{8,10},{10,8},{9,1... | collective-permute-start | bytes 3932168 | tf_op jit(solution)/shard_map/ppermute | solution.py:19
  789.2 2.2 collective-permute-start.7
where the time goes:
time: 793 us; the launch traced here: 792 us
  waiting for transfers between devices  668 us (84%)
  matrix products  61.6 us (8%)
  blocking collectives  34.9 us (4%)
  other arithmetic  24.2 us (3%)
    ppermute x8, waiting for transfers between devices, partner(): return lax.ppermute(block, axis, route)  668 us
    psum x1, blocking collectives, per_device(): totals = lax.psum(jnp.sum(narrowed * narrowed, axis=1), 'gx')  34.9 us
    dot_general x1, matrix products, per_device(): jnp.dot(hidden, down_tile, preferred_element_type=jnp.float32)  21.8 us
    dot_general x1, matrix products, per_device(): gate_part = jnp.dot(block, gate_tile, preferred_element_type=jnp.float32)  21.7 us
    dot_general x1, matrix products, per_device(): up_part = jnp.dot(block, up_tile, preferred_element_type=jnp.float32)  18.1 us
  transfers between devices with their start and end apart: 8, of which 8 were waited for; matrix products, arithmetic and copies ran while one was open for 0% of the time, Pallas kernels for 0%

commit v1 on v0

v1 whole, which is shorter than its diff:
```python
import functools

import jax
import jax.numpy as jnp
from jax import lax
from jax.experimental import pallas as pl
from jax.experimental.pallas import tpu as pltpu
from jax.sharding import PartitionSpec as P

epsilon = 1e-05
F32 = jnp.float32
BF16 = jnp.bfloat16

UNIT_CHUNK = 128
LAG = 2
SLOTS = 3
GAIN_ROWS = 16


def slab_kernel(n, feat_split, features, x_ref, gate_ref, up_ref, down_ref, out_ref,
                raw, square_part, square_block, normed, acc, fresh, parts, hidden,
                wide_tile, down_tile, sib_out, sib_in, row_out, row_in,
                raw_send, raw_recv, pass_send, pass_recv, sq_send, sq_recv, sb_send, sb_recv,
                part_send, part_recv, hid_send, hid_recv, wide_sem, down_sem,
                sib_send, sib_recv, row_send, row_recv):
    R = feat_split
    U = n // R
    H = U // 2
    rows = out_ref.shape[0]
    w = out_ref.shape[1]
    units = gate_ref.shape[2]
    CH = UNIT_CHUNK
    K = units // 2 // CH

    me = lax.axis_index("gx")
    r = me // U
    c = me % U
    h = c // 2
    s = c % 2
    base = me - c
    sibling = base + 2 * h + 1 - s

    def at(index):
        return {"gx": index}

    def remote(src, dst, send, recv, target):
        return pltpu.make_async_remote_copy(
            src_ref=src, dst_ref=dst, send_sem=send, recv_sem=recv,
            device_id=at(target), device_id_type=pl.DeviceIdType.MESH)

    def wide_copies(d, k):
        slot = k % SLOTS
        start = pl.multiple_of(d * (units // 2) + k * CH, CH)
        return [
            pltpu.make_async_copy(ref.at[0, :, pl.ds(start, CH)],
                                  wide_tile.at[d, slot, :, pl.ds(i * CH, CH)],
                                  wide_sem.at[d, slot, i])
            for i, ref in enumerate((gate_ref, up_ref))
        ]

    def down_copy(d, k):
        slot = k % SLOTS
        start = pl.multiple_of(d * (units // 2) + k * CH, CH)
        return pltpu.make_async_copy(down_ref.at[0, pl.ds(start, CH), :],
                                     down_tile.at[d, slot], down_sem.at[d, slot])

    for k in range(min(SLOTS, K)):
        for d in range(2):
            for copy in wide_copies(d, k):
                copy.start()
            down_copy(d, k).start()

    barrier = pltpu.get_barrier_semaphore()
    for i in range(1, U):
        pl.semaphore_signal(barrier, inc=1, device_id=at(base + (c + i) % U),
                            device_id_type=pl.DeviceIdType.MESH)
    for i in range(1, R):
        pl.semaphore_signal(barrier, inc=1, device_id=at((me + i * U) % n),
                            device_id_type=pl.DeviceIdType.MESH)
    pl.semaphore_wait(barrier, U - 1 + R - 1)

    def raw_copy(i):
        target = sibling if i == 0 else base + 2 * ((h + i) % H) + s
        return remote(x_ref, raw.at[c], raw_send.at[i], raw_recv.at[i], target)

    def pass_copy(i):
        source = 2 * ((h + H - i) % H) + s
        return remote(raw.at[source], raw.at[source], pass_send.at[i], pass_recv.at[i], sibling)

    for i in range(1, H):
        raw_copy(i).start()
    raw_copy(0).start()

    own = x_ref[:rows, :].astype(F32)
    column = jnp.sum(own * own, axis=1, keepdims=True)
    eye = (lax.broadcasted_iota(jnp.int32, (rows, rows), 0)
           == lax.broadcasted_iota(jnp.int32, (rows, rows), 1))
    square_part[c] = jnp.broadcast_to(
        jnp.sum(jnp.where(eye, column, 0.0), axis=0, keepdims=True), (8, rows))

    def sq_copy(i):
        return remote(square_part.at[c], square_part.at[c], sq_send.at[i], sq_recv.at[i],
                      base + (c + i) % U)

    for i in range(1, U):
        sq_copy(i).start()
    raw[c] = x_ref[...]
    acc[...] = jnp.zeros_like(acc)
    for i in range(1, U):
        sq_copy(i).wait()
    square_block[r] = jnp.sum(square_part[...], axis=0)

    def sb_copy(i):
        return remote(square_block.at[r], square_block.at[r], sb_send.at[i], sb_recv.at[i],
                      (me + i * U) % n)

    for i in range(1, R):
        sb_copy(i).start()
    for i in range(1, R):
        sb_copy(i).wait()
    total = jnp.sum(square_block[...], axis=0)[0:1, :]
    total = jnp.sum(jnp.where(eye, total, 0.0), axis=1, keepdims=True)
    scaling = lax.rsqrt(total / features + epsilon)

    for i in range(1, H):
        raw_copy(i).wait_recv()
        pass_copy(i).start()
    raw_copy(0).wait_recv()
    for i in range(1, H):
        pass_copy(i).wait_recv()
    for j in range(U):
        gain = raw[j, rows:, :].astype(F32)[0:1, :]
        block = raw[j, :rows, :].astype(F32)
        normed[:, j * w:(j + 1) * w] = (block * scaling * gain).astype(BF16)
    for i in range(H):
        raw_copy(i).wait_send()
    for i in range(1, H):
        pass_copy(i).wait_send()

    position = (r, R - 1 - r)
    ahead = ((me + U) % n, (me + n - U) % n)
    behind = ((me + n - U) % n, (me + U) % n)

    def part_copy(d, k):
        return remote(parts.at[d, k], parts.at[d, k], part_send.at[d, k], part_recv.at[d, k],
                      ahead[d])

    def hid_copy(d, k):
        return remote(hidden.at[d, k], hidden.at[d, k], hid_send.at[d, k], hid_recv.at[d, k],
                      behind[d])

    def step(t, carry):
        for d in range(2):
            pos = position[d]
            kh = t - LAG * (R - 1) - LAG * (R - 1 - pos)

            @pl.when((kh >= 0) & (kh < K) & (pos < R - 1))
            def _():
                hid_copy(d, kh).wait_recv()

                @pl.when(pos > 0)
                def _():
                    hid_copy(d, kh).start()

        for d in range(2):
            pos = position[d]
            kp = t - LAG * pos

            @pl.when((kp >= 0) & (kp < K))
            def _():
                for copy in wide_copies(d, kp):
                    copy.wait()
                fresh[d] = jnp.dot(normed[...], wide_tile[d, kp % SLOTS],
                                   preferred_element_type=F32)

                @pl.when(kp + SLOTS < K)
                def _():
                    for copy in wide_copies(d, kp + SLOTS):
                        copy.start()

                @pl.when(pos == 0)
                def _():
                    parts[d, kp] = fresh[d].astype(BF16)

                @pl.when(pos > 0)
                def _():
                    part_copy(d, kp).wait_recv()

                @pl.when((pos > 0) & (pos < R - 1))
                def _():
                    parts[d, kp] = (fresh[d] + parts[d, kp].astype(F32)).astype(BF16)

                @pl.when(pos < R - 1)
                def _():
                    part_copy(d, kp).start()

                @pl.when(pos == R - 1)
                def _():
                    whole = fresh[d] + parts[d, kp].astype(F32)
                    gate = whole[:, :CH]
                    hidden[d, kp] = (gate / (1.0 + jnp.exp(-gate)) * whole[:, CH:]).astype(BF16)
                    hid_copy(d, kp).start()

        for d in range(2):
            pos = position[d]
            kh = t - LAG * (R - 1) - LAG * (R - 1 - pos)

            @pl.when((kh >= 0) & (kh < K))
            def _():
                down_copy(d, kh).wait()
                value = hidden[d, kh]
                for j in range(U):
                    acc[j] += jnp.dot(value, down_tile[d, kh % SLOTS, :, j * w:(j + 1) * w],
                                      preferred_element_type=F32)

                @pl.when(kh + SLOTS < K)
                def _():
                    down_copy(d, kh + SLOTS).start()
        return carry

    lax.fori_loop(0, K + 2 * LAG * (R - 1), step, 0)

    def sib_copy(i):
        other = (h + i) % H
        return remote(sib_out.at[other], sib_in.at[other], sib_send.at[i], sib_recv.at[i], sibling)

    def row_copy(i):
        return remote(row_out.at[i], row_in.at[i], row_send.at[i], row_recv.at[i],
                      base + 2 * ((h + i) % H) + s)

    for i in list(range(1, H)) + [0]:
        other = (h + i) % H
        sib_out[other] = acc[2 * other + 1 - s].astype(BF16)
        sib_copy(i).start()
    for i in range(1, H):
        other = (h + i) % H
        sib_copy(i).wait_recv()
        row_out[i] = (acc[2 * other + s] + sib_in[other].astype(F32)).astype(BF16)
        row_copy(i).start()

    def drain(k, carry):
        for d in range(2):
            pos = position[d]

            @pl.when(pos < R - 1)
            def _():
                part_copy(d, k).wait_send()

            @pl.when(pos > 0)
            def _():
                hid_copy(d, k).wait_send()
        return carry

    lax.fori_loop(0, K, drain, 0)
    sib_copy(0).wait_recv()
    result = acc[2 * h + s] + sib_in[h].astype(F32)
    for i in range(1, H):
        row_copy(i).wait_recv()
        result = result + row_in[i].astype(F32)
    out_ref[...] = result.astype(BF16)
    for i in range(H):
        sib_copy(i).wait_send()
    for i in range(1, H):
        row_copy(i).wait_send()


def per_device(n, tokens, norm_gain, gate_weight, up_weight, down_weight):
    rows, w = tokens.shape
    features = w * n
    feat = gate_weight.shape[1]
    units = gate_weight.shape[2]
    R = features // feat
    U = n // R
    H = U // 2
    K = units // 2 // UNIT_CHUNK
    x = jnp.concatenate([tokens, jnp.broadcast_to(norm_gain[None, :], (GAIN_ROWS, w))], 0)
    dma = pltpu.SemaphoreType.DMA
    vmem = pl.BlockSpec(memory_space=pltpu.VMEM)
    anywhere = pl.BlockSpec(memory_space=pl.ANY)
    return pl.pallas_call(
        functools.partial(slab_kernel, n, R, features),
        out_shape=jax.ShapeDtypeStruct((rows, w), BF16),
        in_specs=[vmem, anywhere, anywhere, anywhere],
        out_specs=vmem,
        scratch_shapes=[
            pltpu.VMEM((U, rows + GAIN_ROWS, w), BF16),
            pltpu.VMEM((U, 8, rows), F32),
            pltpu.VMEM((R, 8, rows), F32),
            pltpu.VMEM((rows, feat), BF16),
            pltpu.VMEM((U, rows, w), F32),
            pltpu.VMEM((2, rows, 2 * UNIT_CHUNK), F32),
            pltpu.VMEM((2, K, rows, 2 * UNIT_CHUNK), BF16),
            pltpu.VMEM((2, K, rows, UNIT_CHUNK), BF16),
            pltpu.VMEM((2, SLOTS, feat, 2 * UNIT_CHUNK), BF16),
            pltpu.VMEM((2, SLOTS, UNIT_CHUNK, feat), BF16),
            pltpu.VMEM((H, rows, w), BF16),
            pltpu.VMEM((H, rows, w), BF16),
            pltpu.VMEM((H, rows, w), BF16),
            pltpu.VMEM((H, rows, w), BF16),
            dma((H,)), dma((H,)), dma((H,)), dma((H,)),
            dma((U,)), dma((U,)), dma((R,)), dma((R,)),
            dma((2, K)), dma((2, K)), dma((2, K)), dma((2, K)),
            dma((2, SLOTS, 2)), dma((2, SLOTS)),
            dma((H,)), dma((H,)), dma((H,)), dma((H,)),
        ],
        compiler_params=pltpu.CompilerParams(
            collective_id=0, has_side_effects=True, vmem_limit_bytes=52 * 2**20),
        cost_estimate=pl.CostEstimate(
            flops=6 * rows * feat * units, bytes_accessed=6 * feat * units,
            transcendentals=rows * units),
    )(x, gate_weight, up_weight, down_weight)


def solution(mesh):
    placed = (
        P("groups", "gx"),
        P("gx"),
        P("gx", None, None),
        P("gx", None, None),
        P("gx", None, None),
    )
    return jax.shard_map(
        functools.partial(per_device, mesh.shape["gx"]),
        mesh=mesh, in_specs=placed, out_specs=P("groups", "gx"), check_vma=False,
    )
```

time: 793 us -> 203 us (0.26)
  waiting for transfers between devices: 668 us -> 0 us
  Pallas kernels: 0 us -> 200 us
  matrix products: 61.6 us -> 0 us
  blocking collectives: 34.9 us -> 0 us
  other arithmetic: 24.2 us -> 0.99 us
    ppermute x8 -> x0, waiting for transfers between devices: 668 us -> none  [partner(): return lax.ppermute(block, axis, route)]
    pallas_call x0 -> x1, Pallas kernels: none -> 200 us  [per_device(): pl.pallas_call(functools.partial(slab_kernel, n, R, features), out_shape=...]
    dot_general x3 -> x0, matrix products: 61.6 us -> none  [the longest x1 21.8 us: per_device(): jnp.dot(hidden, down_tile, preferred_element_type=jnp.float32)]
    psum x1 -> x0, blocking collectives: 34.9 us -> none  [per_device(): totals = lax.psum(jnp.sum(narrowed * narrowed, axis=1), 'gx')]
    add x3 -> x0, other arithmetic: 11.4 us -> none  [the longest x2 11 us: per_device(): stacked = keeping + partner(sending, 'gx', bit)]
    select_n x6 -> x0, other arithmetic: 8.29 us -> none  [the longest x4 7.58 us: per_device(): sending = jnp.where(upper, lower_half, upper_half)]
  transfers between devices with their start and end apart: 8 -> 0, of which waited for: 8 -> 0; matrix products, arithmetic and copies ran while one was open for 0% -> 0% of each run, Pallas kernels for 0% -> 0%
where the time goes in v1:
time: 203 us
  Pallas kernels  200 us (99%)
    pallas_call x1, Pallas kernels, per_device(): pl.pallas_call(functools.partial(slab_kernel, n, R, features), out_shape=...  200 us

profile of v1, /device:TPU:0, one launch (start us, length us, event | category | flops | bytes accessed | tf_op | source)
XLA Modules:
  0.0 202.7 jit_solution(8357242913229308406)
XLA Ops:
  0.0 0.7 broadcast_in_dim.2
  0.7 1.0 pad_maximum_fusion.x_ref
  1.7 200.2 %shard_map.55 = bf16[320,512]{1,0:T(8,128)(2,1)S(1)} custom-call(bf16[336,512]{1,0:T(8,128)(2,1)S(1)} %pad_maximum_fusion.x_ref, bf16[1,2048,7168]{2,1,0:T(8,128)(2,1)} %gate_ref.1, bf16[1,2048,7168]{2,1,0:T(8,128)(2,1)} %up_ref.1, bf16[1,7168,2048]{2,1,0:T(8,128)(2,1)} %down_ref.1), custom_call_target="tpu_custom_call" | custom-call | flops 28185722880 | bytes 88080384 | tf_op jit(solution)/shard_map/pallas_call | solution.py:280
  201.9 0.7 copy.7

commit v2 on v1

v2 whole, which is shorter than its diff:
```python
import functools

import jax
import jax.numpy as jnp
from jax import lax
from jax.experimental import pallas as pl
from jax.experimental.pallas import tpu as pltpu
from jax.sharding import PartitionSpec as P

epsilon = 1e-05
F32 = jnp.float32
BF16 = jnp.bfloat16

UNIT_CHUNK = 256
ROW_SPLIT = 2
LAG = 2
SLOTS = 3
GAIN_ROWS = 16


def chunk_of(units):
    return UNIT_CHUNK if units // 2 % UNIT_CHUNK == 0 else 128


def slab_kernel(n, feat_split, features, x_ref, gate_ref, up_ref, down_ref, out_ref,
                raw, square_part, square_block, scale, normed, acc, fresh, parts, hidden,
                wide_tile, down_tile, sib_out, sib_in, row_out, row_in,
                raw_send, raw_recv, pass_send, pass_recv, sq_send, sq_recv, sb_send, sb_recv,
                part_send, part_recv, hid_send, hid_recv, wide_sem, down_sem,
                sib_send, sib_recv, row_send, row_recv):
    R = feat_split
    U = n // R
    H = U // 2
    Q = ROW_SPLIT
    rows = out_ref.shape[0]
    part = rows // Q
    w = out_ref.shape[1]
    units = gate_ref.shape[2]
    CH = chunk_of(units)
    KU = units // 2 // CH
    K = Q * KU
    T = K + 2 * LAG * (R - 1)

    me = lax.axis_index("gx")
    r = me // U
    c = me % U
    h = c // 2
    s = c % 2
    base = me - c
    sibling = base + 2 * h + 1 - s

    def at(index):
        return {"gx": index}

    def remote(src, dst, send, recv, target):
        return pltpu.make_async_remote_copy(
            src_ref=src, dst_ref=dst, send_sem=send, recv_sem=recv,
            device_id=at(target), device_id_type=pl.DeviceIdType.MESH)

    def wide_copies(d, k):
        slot = k % SLOTS
        start = pl.multiple_of(d * (units // 2) + k % KU * CH, CH)
        return [
            pltpu.make_async_copy(ref.at[0, :, pl.ds(start, CH)],
                                  wide_tile.at[d, slot, :, pl.ds(i * CH, CH)],
                                  wide_sem.at[d, slot, i])
            for i, ref in enumerate((gate_ref, up_ref))
        ]

    def down_copy(d, k):
        slot = k % SLOTS
        start = pl.multiple_of(d * (units // 2) + k % KU * CH, CH)
        return pltpu.make_async_copy(down_ref.at[0, pl.ds(start, CH), :],
                                     down_tile.at[d, slot], down_sem.at[d, slot])

    for k in range(min(SLOTS, K)):
        for d in range(2):
            for copy in wide_copies(d, k):
                copy.start()
            down_copy(d, k).start()

    barrier = pltpu.get_barrier_semaphore()
    for i in range(1, U):
        pl.semaphore_signal(barrier, inc=1, device_id=at(base + (c + i) % U),
                            device_id_type=pl.DeviceIdType.MESH)
    for i in range(1, R):
        pl.semaphore_signal(barrier, inc=1, device_id=at((me + i * U) % n),
                            device_id_type=pl.DeviceIdType.MESH)
    pl.semaphore_wait(barrier, U - 1 + R - 1)

    def raw_copy(q, i):
        target = sibling if i == 0 else base + 2 * ((h + i) % H) + s
        return remote(x_ref.at[q], raw.at[q, c], raw_send.at[q, i], raw_recv.at[q, i], target)

    def pass_copy(q, i):
        source = 2 * ((h + H - i) % H) + s
        return remote(raw.at[q, source], raw.at[q, source], pass_send.at[q, i],
                      pass_recv.at[q, i], sibling)

    def pass_on(q):
        for i in range(1, H):
            raw_copy(q, i).wait_recv()
            pass_copy(q, i).start()

    def normalise(q):
        raw_copy(q, 0).wait_recv()
        for i in range(1, H):
            pass_copy(q, i).wait_recv()
        for j in range(U):
            gain = raw[q, j, part:, :].astype(F32)[0:1, :]
            block = raw[q, j, :part, :].astype(F32)
            normed[q, :, j * w:(j + 1) * w] = (
                block * scale[q * part:(q + 1) * part, :] * gain).astype(BF16)
        for i in range(H):
            raw_copy(q, i).wait_send()
        for i in range(1, H):
            pass_copy(q, i).wait_send()

    for q in range(Q):
        for i in range(1, H):
            raw_copy(q, i).start()
        raw_copy(q, 0).start()

    column = []
    for q in range(Q):
        own = x_ref[q, :part, :].astype(F32)
        column.append(jnp.sum(own * own, axis=1, keepdims=True))
    column = jnp.concatenate(column, axis=0)
    eye = (lax.broadcasted_iota(jnp.int32, (rows, rows), 0)
           == lax.broadcasted_iota(jnp.int32, (rows, rows), 1))
    square_part[c] = jnp.broadcast_to(
        jnp.sum(jnp.where(eye, column, 0.0), axis=0, keepdims=True), (8, rows))

    def sq_copy(i):
        return remote(square_part.at[c], square_part.at[c], sq_send.at[i], sq_recv.at[i],
                      base + (c + i) % U)

    for i in range(1, U):
        sq_copy(i).start()
    for q in range(Q):
        raw[q, c] = x_ref[q]
    acc[...] = jnp.zeros_like(acc)
    for i in range(1, U):
        sq_copy(i).wait()
    square_block[r] = jnp.sum(square_part[...], axis=0)

    def sb_copy(i):
        return remote(square_block.at[r], square_block.at[r], sb_send.at[i], sb_recv.at[i],
                      (me + i * U) % n)

    for i in range(1, R):
        sb_copy(i).start()
    for i in range(1, R):
        sb_copy(i).wait()
    total = jnp.sum(square_block[...], axis=0)[0:1, :]
    total = jnp.sum(jnp.where(eye, total, 0.0), axis=1, keepdims=True)
    scale[...] = lax.rsqrt(total / features + epsilon)
    pass_on(0)
    normalise(0)

    position = (r, R - 1 - r)
    ahead = ((me + U) % n, (me + n - U) % n)
    behind = ((me + n - U) % n, (me + U) % n)

    def part_copy(d, k):
        return remote(parts.at[d, k], parts.at[d, k], part_send.at[d, k], part_recv.at[d, k],
                      ahead[d])

    def hid_copy(d, k):
        return remote(hidden.at[d, k], hidden.at[d, k], hid_send.at[d, k], hid_recv.at[d, k],
                      behind[d])

    def sib_copy(q, i):
        other = (h + i) % H
        return remote(sib_out.at[q, other], sib_in.at[q, other], sib_send.at[q, i],
                      sib_recv.at[q, i], sibling)

    def row_copy(q, i):
        return remote(row_out.at[q, i], row_in.at[q, i], row_send.at[q, i], row_recv.at[q, i],
                      base + 2 * ((h + i) % H) + s)

    def to_sibling(q):
        for i in list(range(1, H)) + [0]:
            other = (h + i) % H
            sib_out[q, other] = acc[q, 2 * other + 1 - s].astype(BF16)
            sib_copy(q, i).start()

    def to_chips(q):
        for i in range(1, H):
            other = (h + i) % H
            sib_copy(q, i).wait_recv()
            row_out[q, i] = (acc[q, 2 * other + s] + sib_in[q, other].astype(F32)).astype(BF16)
            row_copy(q, i).start()

    def finish(q):
        sib_copy(q, 0).wait_recv()
        result = acc[q, 2 * h + s] + sib_in[q, h].astype(F32)
        for i in range(1, H):
            row_copy(q, i).wait_recv()
            result = result + row_in[q, i].astype(F32)
        out_ref[q * part:(q + 1) * part, :] = result.astype(BF16)
        for i in range(H):
            sib_copy(q, i).wait_send()
        for i in range(1, H):
            row_copy(q, i).wait_send()

    def step(t, carry):
        for q in range(1, Q):
            @pl.when(t == q * KU - 6)
            def _():
                pass_on(q)

            @pl.when(t == q * KU - 3)
            def _():
                normalise(q)

            @pl.when(t == q * KU + 2 * LAG * (R - 1))
            def _():
                to_sibling(q - 1)

            @pl.when(t == q * KU + 2 * LAG * (R - 1) + 2)
            def _():
                to_chips(q - 1)

        for d in range(2):
            kp = t - LAG * position[d]

            @pl.when((kp >= 0) & (kp < K))
            def _():
                for copy in wide_copies(d, kp):
                    copy.wait()
                fresh[d] = jnp.dot(normed[kp // KU], wide_tile[d, kp % SLOTS],
                                   preferred_element_type=F32)

                @pl.when(kp + SLOTS < K)
                def _():
                    for copy in wide_copies(d, kp + SLOTS):
                        copy.start()

        for d in range(2):
            pos = position[d]
            kh = t - LAG * (R - 1) - LAG * (R - 1 - pos)
            kp = t - LAG * pos

            @pl.when((kh >= 0) & (kh < K) & (pos < R - 1))
            def _():
                hid_copy(d, kh).wait_recv()

                @pl.when(pos > 0)
                def _():
                    hid_copy(d, kh).start()

            @pl.when((kp >= 0) & (kp < K))
            def _():
                @pl.when(pos == 0)
                def _():
                    parts[d, kp] = fresh[d].astype(BF16)

                @pl.when(pos > 0)
                def _():
                    part_copy(d, kp).wait_recv()

                @pl.when((pos > 0) & (pos < R - 1))
                def _():
                    parts[d, kp] = (fresh[d] + parts[d, kp].astype(F32)).astype(BF16)

                @pl.when(pos < R - 1)
                def _():
                    part_copy(d, kp).start()

                @pl.when(pos == R - 1)
                def _():
                    whole = fresh[d] + parts[d, kp].astype(F32)
                    gate = whole[:, :CH]
                    hidden[d, kp] = (gate / (1.0 + jnp.exp(-gate)) * whole[:, CH:]).astype(BF16)
                    hid_copy(d, kp).start()

        for d in range(2):
            kh = t - LAG * (R - 1) - LAG * (R - 1 - position[d])

            @pl.when((kh >= 0) & (kh < K))
            def _():
                down_copy(d, kh).wait()
                value = hidden[d, kh]
                for j in range(U):
                    acc[kh // KU, j] += jnp.dot(
                        value, down_tile[d, kh % SLOTS, :, j * w:(j + 1) * w],
                        preferred_element_type=F32)

                @pl.when(kh + SLOTS < K)
                def _():
                    down_copy(d, kh + SLOTS).start()
        return carry

    lax.fori_loop(0, T, step, 0)
    to_sibling(Q - 1)
    to_chips(Q - 1)

    def drain(k, carry):
        for d in range(2):
            pos = position[d]

            @pl.when(pos < R - 1)
            def _():
                part_copy(d, k).wait_send()

            @pl.when(pos > 0)
            def _():
                hid_copy(d, k).wait_send()
        return carry

    lax.fori_loop(0, K, drain, 0)
    for q in range(Q):
        finish(q)


def per_device(n, tokens, norm_gain, gate_weight, up_weight, down_weight):
    rows, w = tokens.shape
    features = w * n
    feat = gate_weight.shape[1]
    units = gate_weight.shape[2]
    R = features // feat
    U = n // R
    H = U // 2
    Q = ROW_SPLIT
    part = rows // Q
    CH = chunk_of(units)
    K = Q * (units // 2 // CH)
    x = jnp.concatenate([tokens.reshape(Q, part, w),
                         jnp.broadcast_to(norm_gain[None, None, :], (Q, GAIN_ROWS, w))], 1)
    dma = pltpu.SemaphoreType.DMA
    vmem = pl.BlockSpec(memory_space=pltpu.VMEM)
    anywhere = pl.BlockSpec(memory_space=pl.ANY)
    return pl.pallas_call(
        functools.partial(slab_kernel, n, R, features),
        out_shape=jax.ShapeDtypeStruct((rows, w), BF16),
        in_specs=[vmem, anywhere, anywhere, anywhere],
        out_specs=vmem,
        scratch_shapes=[
            pltpu.VMEM((Q, U, part + GAIN_ROWS, w), BF16),
            pltpu.VMEM((U, 8, rows), F32),
            pltpu.VMEM((R, 8, rows), F32),
            pltpu.VMEM((rows, 1), F32),
            pltpu.VMEM((Q, part, feat), BF16),
            pltpu.VMEM((Q, U, part, w), F32),
            pltpu.VMEM((2, part, 2 * CH), F32),
            pltpu.VMEM((2, K, part, 2 * CH), BF16),
            pltpu.VMEM((2, K, part, CH), BF16),
            pltpu.VMEM((2, SLOTS, feat, 2 * CH), BF16),
            pltpu.VMEM((2, SLOTS, CH, feat), BF16),
            pltpu.VMEM((Q, H, part, w), BF16),
            pltpu.VMEM((Q, H, part, w), BF16),
            pltpu.VMEM((Q, H, part, w), BF16),
            pltpu.VMEM((Q, H, part, w), BF16),
            dma((Q, H)), dma((Q, H)), dma((Q, H)), dma((Q, H)),
            dma((U,)), dma((U,)), dma((R,)), dma((R,)),
            dma((2, K)), dma((2, K)), dma((2, K)), dma((2, K)),
            dma((2, SLOTS, 2)), dma((2, SLOTS)),
            dma((Q, H)), dma((Q, H)), dma((Q, H)), dma((Q, H)),
        ],
        compiler_params=pltpu.CompilerParams(
            collective_id=0, has_side_effects=True, vmem_limit_bytes=52 * 2**20),
        cost_estimate=pl.CostEstimate(
            flops=6 * rows * feat * units, bytes_accessed=6 * feat * units,
            transcendentals=rows * units),
    )(x, gate_weight, up_weight, down_weight)


def solution(mesh):
    placed = (
        P("groups", "gx"),
        P("gx"),
        P("gx", None, None),
        P("gx", None, None),
        P("gx", None, None),
    )
    return jax.shard_map(
        functools.partial(per_device, mesh.shape["gx"]),
        mesh=mesh, in_specs=placed, out_specs=P("groups", "gx"), check_vma=False,
    )
```

time: 203 us -> 198 us (0.975)
  Pallas kernels: 200 us -> 195 us
    pallas_call x1, Pallas kernels: 200 us -> 195 us  [per_device(): pl.pallas_call(functools.partial(slab_kernel, n, R, features), out_shape=...]
where the time goes in v2:
time: 198 us
  Pallas kernels  195 us (98%)
    pallas_call x1, Pallas kernels, per_device(): pl.pallas_call(functools.partial(slab_kernel, n, R, features), out_shape=...  195 us

profile of v2, /device:TPU:0, one launch (start us, length us, event | category | flops | bytes accessed | tf_op | source)
XLA Modules:
  0.0 197.6 jit_solution(6204404567535733798)
XLA Ops:
  0.0 0.7 broadcast_in_dim.2
  0.7 1.0 pad_maximum_fusion.x_ref
  1.7 195.2 %shard_map.55 = bf16[320,512]{1,0:T(8,128)(2,1)S(1)} custom-call(bf16[2,176,512]{2,1,0:T(8,128)(2,1)S(1)} %pad_maximum_fusion.x_ref, bf16[1,2048,7168]{2,1,0:T(8,128)(2,1)} %gate_ref.1, bf16[1,2048,7168]{2,1,0:T(8,128)(2,1)} %up_ref.1, bf16[1,7168,2048]{2,1,0:T(8,128)(2,1)} %down_ref.1), custom_call_target="tpu_custom_call" | custom-call | flops 28185722880 | bytes 88080384 | tf_op jit(solution)/shard_map/pallas_call | solution.py:334
  196.8 0.7 copy.7
